TPU v7x, 32 devices: a whole 2x2x4 slice. The times are simulated.
32 devices in a mesh: gx: 4 (over z), gy: 8 (over y, x, core).
Axes of the slice: x: 2, y: 2, z: 4, core: 2. Of those that a mesh axis runs over, the one named last changes fastest.
Arguments:
- start_coeffs: float32 [9, 512, 2048], P(None, 'gy', 'gx'), may hold values from -6 to 6
- section_coeffs: float32 [9, 512, 2048], P(None, 'gy', 'gx'), may hold values from -6 to 6
- vel_x: float32 [512, 2048], P('gy', 'gx'), may hold values from -1 to 1
- vel_y: float32 [512, 2048], P('gy', 'gx'), may hold values from -1 to 1
Outputs:
- updated: float32 [9, 512, 2048], P(None, 'gy', 'gx')
- filtered: float32 [9, 512, 2048], P(None, 'gy', 'gx')
All inputs are finite; a program needn't handle non-finite values.
Results may differ from a plain program's by a relative error of at most 0.0001.
Values sent between devices are 32-bit elements; how exact they have to be, the bound alone decides.
A program may use at most 64 MiB of HBM per device.

v0:
```python
import functools

import jax
import jax.numpy as jnp
import numpy as np
from jax import lax
from jax.experimental import pallas as pl
from jax.experimental.pallas import tpu as pltpu
from jax.sharding import PartitionSpec as P

STEP_SIZE = 0.3
GAUSS_NODES = (
    -0.932469514203152,
    -0.6612093864662645,
    -0.2386191860831969,
    0.2386191860831969,
    0.6612093864662645,
    0.932469514203152,
)
GAUSS_WEIGHTS = (
    0.1713244923791704,
    0.3607615730481386,
    0.467913934572691,
    0.467913934572691,
    0.3607615730481386,
    0.1713244923791704,
)


def legendre_rows(points):
    return np.stack([points * 0.0 + 1.0, points, 1.5 * points * points - 0.5])


def bspline(points):
    magnitude = np.abs(points)
    return np.where(
        magnitude <= 0.5,
        0.75 - magnitude * magnitude,
        np.where(magnitude <= 1.5, 0.5 * (1.5 - magnitude) ** 2, 0.0),
    )


def kernel_value(points):
    return 1.25 * bspline(points) - 0.125 * (bspline(points + 1.0) + bspline(points - 1.0))


def siac_table():
    nodes = np.array(GAUSS_NODES)
    weights = np.array(GAUSS_WEIGHTS)
    kernel_table = np.zeros((5, 3, 3))
    for slot_index in range(5):
        offset = slot_index - 2
        for low_end, high_end in ((-1.0, 0.0), (0.0, 1.0)):
            for node_value, node_weight in zip(GAUSS_NODES, GAUSS_WEIGHTS):
                xi_value = 0.5 * (low_end + high_end) + 0.5 * (high_end - low_end) * node_value
                outer_weight = 0.5 * (high_end - low_end) * node_weight
                breaks = [-1.0, 1.0]
                for spline_knot in (-2.5, -1.5, -0.5, 0.5, 1.5, 2.5):
                    crossing = xi_value - 2.0 * offset - 2.0 * spline_knot
                    if -1.0 < crossing < 1.0:
                        breaks.append(crossing)
                breaks = sorted(breaks)
                for piece_lo, piece_hi in zip(breaks[:-1], breaks[1:]):
                    eta_points = 0.5 * (piece_lo + piece_hi) + 0.5 * (piece_hi - piece_lo) * nodes
                    eta_weights = 0.5 * (piece_hi - piece_lo) * weights
                    samples = (
                        kernel_value(0.5 * xi_value - 0.5 * eta_points - offset) * eta_weights * 0.5
                    )
                    kernel_table[slot_index] += outer_weight * np.outer(
                        legendre_rows(np.array(xi_value)), legendre_rows(eta_points) @ samples
                    )
    return kernel_table * (np.arange(3)[None, :, None] + 0.5)


SUB = 8
LANE = 128
HALO = 3
GROUP = 2 * HALO
MODES = 9
FIELDS = 2 * MODES + 2
VEL_X = 2 * MODES
VEL_Y = 2 * MODES + 1
VMEM_BYTES = 40 * 1024 * 1024


def lanes_of(shape):
    return lax.broadcasted_iota(jnp.int32, shape, len(shape) - 1)


def rows_of(tile):
    return pl.ds(pl.multiple_of(tile * SUB, SUB), SUB)


def shift_rows(low, high, count):
    index = lax.broadcasted_iota(jnp.int32, low.shape, 0)
    return pltpu.roll(jnp.where(index < count, high, low), SUB - count, 0)


def roll_lanes(value, amount):
    width = value.shape[-1]
    return pltpu.roll(value, (-amount) % width, len(value.shape) - 1)


def upwind(speed, inner, outer):
    return jnp.maximum(speed, 0.0) * inner + jnp.minimum(speed, 0.0) * outer


def pack_tile(ext, pack, width, tile):
    rows = rows_of(tile)
    lane = lanes_of((SUB, LANE))
    packed = jnp.zeros((SUB, LANE), jnp.float32)
    for field in range(FIELDS):
        edges = jnp.where(
            lane < LANE // 2, ext[field, rows, 0:LANE], ext[field, rows, width - LANE : width]
        )
        moved = pltpu.roll(edges, (HALO + GROUP * field) % LANE, 1)
        inside = (lane >= GROUP * field) & (lane < GROUP * (field + 1))
        packed = jnp.where(inside, moved, packed)
    pack[rows, :] = packed


def unpack_tile(ext, from_west, from_east, width, tile):
    rows = rows_of(tile)
    lane = lanes_of((SUB, LANE))
    mixed = jnp.where(lax.rem(lane, GROUP) < HALO, from_west[rows, :], from_east[rows, :])
    for field in range(FIELDS):
        ext[field, rows, width : width + LANE] = pltpu.roll(
            mixed, (-(HALO + GROUP * field)) % LANE, 1
        )


def update_tile(ext, out, tiles, tile):
    here = rows_of(tile)
    below = rows_of(lax.rem(tile + (tiles - 1), tiles))
    above = rows_of(lax.rem(tile + 1, tiles))
    coeffs = [[ext[3 * i + j, here, :] for j in range(3)] for i in range(3)]
    vel_x = ext[VEL_X, here, :]
    vel_y = ext[VEL_Y, here, :]
    rate = [[None] * 3 for _ in range(3)]
    speed = 0.5 * (vel_x + roll_lanes(vel_x, 1))
    up, down = jnp.maximum(speed, 0.0), jnp.minimum(speed, 0.0)
    scale = STEP_SIZE * 2.0 / 3.0
    for j in range(3):
        even = coeffs[0][j] + coeffs[2][j]
        east_face = up * (even + coeffs[1][j]) + down * roll_lanes(even - coeffs[1][j], 1)
        west_face = roll_lanes(east_face, -1)
        change = east_face - west_face
        total = east_face + west_face
        rate[0][j] = (-0.5 * scale) * change
        rate[1][j] = (1.5 * scale) * (2.0 * vel_x * coeffs[0][j] - total)
        rate[2][j] = (2.5 * scale) * (2.0 * vel_x * coeffs[1][j] - change)
    speed_n = 0.5 * (vel_y + shift_rows(vel_y, ext[VEL_Y, above, :], 1))
    speed_s = 0.5 * (vel_y + shift_rows(ext[VEL_Y, below, :], vel_y, SUB - 1))
    up_n, down_n = jnp.maximum(speed_n, 0.0), jnp.minimum(speed_n, 0.0)
    up_s, down_s = jnp.maximum(speed_s, 0.0), jnp.minimum(speed_s, 0.0)
    for i in range(3):
        even = coeffs[i][0] + coeffs[i][2]
        north = even + coeffs[i][1]
        south = even - coeffs[i][1]
        south_above = ext[3 * i, above, :] - ext[3 * i + 1, above, :] + ext[3 * i + 2, above, :]
        north_below = ext[3 * i, below, :] + ext[3 * i + 1, below, :] + ext[3 * i + 2, below, :]
        north_face = up_n * north + down_n * shift_rows(south, south_above, 1)
        south_face = up_s * shift_rows(north_below, north, SUB - 1) + down_s * south
        change = north_face - south_face
        total = north_face + south_face
        along_y = (
            (-0.5 * scale) * change,
            (1.5 * scale) * (2.0 * vel_y * coeffs[i][0] - total),
            (2.5 * scale) * (2.0 * vel_y * coeffs[i][1] - change),
        )
        for j in range(3):
            mode = 3 * i + j
            out[mode, here, :] = (
                (1.0 / 3.0) * ext[MODES + mode, here, :]
                + (2.0 / 3.0) * coeffs[i][j]
                + (rate[i][j] + along_y[j])
            )


def advance_kernel(
    counts, start, section, vel_x, vel_y, out, ext, pack, from_west, from_east,
    load_sem, send_sem, recv_sem,
):
    height, width = vel_x.shape
    tiles = height // SUB + 1
    me_x, me_y = lax.axis_index("gx"), lax.axis_index("gy")

    def at(step_x, step_y):
        return {
            "gx": lax.rem(me_x + (step_x + counts[0]), counts[0]),
            "gy": lax.rem(me_y + (step_y + counts[1]), counts[1]),
        }

    inner = (pl.ds(0, height), pl.ds(0, width))
    sources = (
        (section, ext.at[(pl.ds(0, MODES),) + inner]),
        (start, ext.at[(pl.ds(MODES, MODES),) + inner]),
        (vel_x, ext.at[(VEL_X,) + inner]),
        (vel_y, ext.at[(VEL_Y,) + inner]),
    )
    loads = [
        pltpu.make_async_copy(source, target, load_sem.at[index])
        for index, (source, target) in enumerate(sources)
    ]
    for load in loads:
        load.start()

    around = [(i, j) for i in (-1, 0, 1) for j in (-1, 0, 1) if (i, j) != (0, 0)]
    barrier = pltpu.get_barrier_semaphore()
    for i, j in around:
        pl.semaphore_signal(
            barrier, inc=1, device_id=at(i, j), device_id_type=pl.DeviceIdType.MESH
        )
    pl.semaphore_wait(barrier, len(around))

    made = []

    def send(source, target, to):
        index = len(made)
        copy = pltpu.make_async_remote_copy(
            src_ref=source,
            dst_ref=target,
            send_sem=send_sem.at[index],
            recv_sem=recv_sem.at[index],
            device_id=to,
            device_id_type=pl.DeviceIdType.MESH,
        )
        copy.start()
        made.append(copy)

    low, high = pl.ds(0, HALO), pl.ds(height - HALO, HALO)
    north_halo, south_halo = pl.ds(height, HALO), pl.ds(height + SUB - HALO, HALO)
    wide = pl.ds(0, width)
    for rows, halo, step in ((low, north_halo, -1), (high, south_halo, 1)):
        send(section.at[:, rows, :], ext.at[pl.ds(0, MODES), halo, wide], at(0, step))
        send(start.at[:, rows, :], ext.at[pl.ds(MODES, MODES), halo, wide], at(0, step))
        send(vel_x.at[rows, :], ext.at[VEL_X, halo, wide], at(0, step))
        send(vel_y.at[rows, :], ext.at[VEL_Y, halo, wide], at(0, step))
    row_copies = list(made)

    for load in loads:
        load.wait()
    pl.loop(0, tiles - 1)(functools.partial(pack_tile, ext, pack, width))
    whole = pl.ds(0, height)
    send(pack.at[whole, :], from_west.at[whole, :], at(1, 0))
    send(pack.at[whole, :], from_east.at[whole, :], at(-1, 0))
    column_copies = made[len(row_copies) :]
    for rows, halo, step in ((low, north_halo, -1), (high, south_halo, 1)):
        send(pack.at[rows, :], from_west.at[halo, :], at(1, step))
        send(pack.at[rows, :], from_east.at[halo, :], at(-1, step))
    corner_copies = made[len(row_copies) + 2 :]

    for copy in column_copies:
        copy.wait_recv()
    pl.loop(0, tiles - 1)(functools.partial(unpack_tile, ext, from_west, from_east, width))
    pl.loop(1, tiles - 2)(functools.partial(update_tile, ext, out, tiles))
    for copy in row_copies + corner_copies:
        copy.wait_recv()
    unpack_tile(ext, from_west, from_east, width, tiles - 1)

    @pl.loop(tiles - 2, tiles + 1)
    def _(tile):
        update_tile(ext, out, tiles, lax.rem(tile, tiles))

    for copy in made:
        copy.wait_send()


def combine(table, middle, plus_1, minus_1, plus_2, minus_2):
    sums = []
    even_1 = [p + m for p, m in zip(plus_1, minus_1)]
    odd_1 = [p - m for p, m in zip(plus_1, minus_1)]
    even_2 = [p + m for p, m in zip(plus_2, minus_2)]
    odd_2 = [p - m for p, m in zip(plus_2, minus_2)]
    for to in range(3):
        total = None
        for degree in range(3):
            same = (to + degree) % 2 == 0
            terms = [
                (table[3][to][degree], (even_1 if same else odd_1)[degree]),
                (table[4][to][degree], (even_2 if same else odd_2)[degree]),
            ]
            if same:
                terms.append((table[2][to][degree], middle[degree]))
            for weight, value in terms:
                term = weight * value
                total = term if total is None else total + term
        sums.append(total)
    return sums


def filter_kernel(table, grid, updated, filtered, swept, result, copy_sem, out_sem):
    modes, height, width = updated.shape
    tiles = height // SUB + 1
    keep = pltpu.make_async_copy(
        grid.at[:, pl.ds(0, height), pl.ds(0, width)], updated, copy_sem
    )
    keep.start()

    @pl.loop(0, tiles)
    def _(tile):
        rows = rows_of(tile)
        for j in range(3):
            middle = [grid[3 * i + j, rows, :] for i in range(3)]
            moved = [[roll_lanes(m, k)[:, :width] for m in middle] for k in (1, -1, 2, -2)]
            sums = combine(table, [m[:, :width] for m in middle], *moved)
            for i in range(3):
                swept[3 * i + j, rows, :] = sums[i]

    @pl.loop(0, tiles - 1)
    def _(tile):
        here = rows_of(tile)
        below = rows_of(lax.rem(tile + (tiles - 1), tiles))
        above = rows_of(tile + 1)
        for i in range(3):
            middle = [swept[3 * i + j, here, :] for j in range(3)]
            high = [swept[3 * i + j, above, :] for j in range(3)]
            low = [swept[3 * i + j, below, :] for j in range(3)]
            sums = combine(
                table,
                middle,
                [shift_rows(m, h, 1) for m, h in zip(middle, high)],
                [shift_rows(l, m, SUB - 1) for m, l in zip(middle, low)],
                [shift_rows(m, h, 2) for m, h in zip(middle, high)],
                [shift_rows(l, m, SUB - 2) for m, l in zip(middle, low)],
            )
            for j in range(3):
                result[3 * i + j, here, :] = sums[j]
        pltpu.make_async_copy(
            result.at[:, here, :], filtered.at[:, here, :], out_sem.at[tile]
        ).start()

    @pl.loop(0, tiles - 1)
    def _(tile):
        here = rows_of(tile)
        pltpu.make_async_copy(
            result.at[:, here, :], filtered.at[:, here, :], out_sem.at[tile]
        ).wait()

    keep.wait()


def per_device(counts, start_coeffs, section_coeffs, vel_x, vel_y):
    modes, height, width = start_coeffs.shape
    tall, wide = height + SUB, width + LANE
    anywhere = pl.BlockSpec(memory_space=pl.ANY)
    local = pl.BlockSpec(memory_space=pltpu.VMEM)
    messages = 14
    grid = pl.pallas_call(
        functools.partial(advance_kernel, counts),
        out_shape=jax.ShapeDtypeStruct((modes, tall, wide), jnp.float32),
        in_specs=[anywhere] * 4,
        out_specs=local,
        scratch_shapes=[
            pltpu.VMEM((FIELDS, tall, wide), jnp.float32),
            pltpu.VMEM((height, LANE), jnp.float32),
            pltpu.VMEM((tall, LANE), jnp.float32),
            pltpu.VMEM((tall, LANE), jnp.float32),
            pltpu.SemaphoreType.DMA((4,)),
            pltpu.SemaphoreType.DMA((messages,)),
            pltpu.SemaphoreType.DMA((messages,)),
        ],
        compiler_params=pltpu.CompilerParams(
            collective_id=0, has_side_effects=True, vmem_limit_bytes=VMEM_BYTES
        ),
        name="advance",
    )(start_coeffs, section_coeffs, vel_x, vel_y)
    table = [[[float(v) for v in row] for row in part] for part in siac_table().astype(np.float32)]
    whole = jax.ShapeDtypeStruct((modes, height, width), jnp.float32)
    return pl.pallas_call(
        functools.partial(filter_kernel, table),
        out_shape=(whole, whole),
        in_specs=[local],
        out_specs=(anywhere, anywhere),
        scratch_shapes=[
            pltpu.VMEM((modes, tall, width), jnp.float32),
            pltpu.VMEM((modes, height, width), jnp.float32),
            pltpu.SemaphoreType.DMA,
            pltpu.SemaphoreType.DMA((height // SUB,)),
        ],
        compiler_params=pltpu.CompilerParams(vmem_limit_bytes=VMEM_BYTES),
        name="siac_filter",
    )(grid)


def solution(mesh):
    placed = (P(None, "gy", "gx"), P(None, "gy", "gx"), P("gy", "gx"), P("gy", "gx"))
    counts = (mesh.shape["gx"], mesh.shape["gy"])
    return jax.shard_map(
        functools.partial(per_device, counts),
        mesh=mesh,
        in_specs=placed,
        out_specs=(P(None, "gy", "gx"), P(None, "gy", "gx")),
        check_vma=False,
    )
```

profile of v0, /device:TPU:0, one launch (start us, length us, event | category | flops | bytes accessed | tf_op | source)
XLA Modules:
  0.0 22.4 jit_solution(3633546150525264111)
XLA Ops:
  0.6 0.0 copy-start
  0.6 1.3 %copy-done = f32[9,64,512]{2,1,0:T(8,128)S(1)} copy-done((f32[9,64,512]{2,1,0:T(8,128)S(1)}, f32[9,64,512]{2,1,0:T(8,128)}, u32[]{:S(2)}) %copy-start) | copy-done | bytes 1179672
  1.9 0.0 copy-start.1
  1.9 1.3 %copy-done.1 = f32[9,64,512]{2,1,0:T(8,128)S(1)} copy-done((f32[9,64,512]{2,1,0:T(8,128)S(1)}, f32[9,64,512]{2,1,0:T(8,128)}, u32[]{:S(2)}) %copy-start.1) | copy-done | bytes 1179672
  3.2 0.0 copy-start.2
  3.2 0.9 %copy-done.2 = f32[64,512]{1,0:T(8,128)S(1)} copy-done((f32[64,512]{1,0:T(8,128)S(1)}, f32[64,512]{1,0:T(8,128)}, u32[]{:S(2)}) %copy-start.2) | copy-done | bytes 131096
  4.1 0.0 copy-start.3
  4.1 0.9 %copy-done.3 = f32[64,512]{1,0:T(8,128)S(1)} copy-done((f32[64,512]{1,0:T(8,128)S(1)}, f32[64,512]{1,0:T(8,128)}, u32[]{:S(2)}) %copy-start.3) | copy-done | bytes 131096
  5.0 12.9 %advance.1.grid = f32[9,72,640]{2,1,0:T(8,128)S(1)} custom-call(f32[9,64,512]{2,1,0:T(8,128)S(1)} %copy-done, f32[9,64,512]{2,1,0:T(8,128)S(1)} %copy-done.1, f32[64,512]{1,0:T(8,128)S(1)} %copy-done.2, f32[64,512]{1,0:T(8,128)S(1)} %copy-done.3), custom_call_target="tpu_custom_call" | custom-call | tf_op jit(solution)/shard_map/advance/pallas_call | solution.py:349
  17.9 4.5 %siac_filter.1 = (f32[9,64,512]{2,1,0:T(8,128)}, f32[9,64,512]{2,1,0:T(8,128)}) custom-call(f32[9,72,640]{2,1,0:T(8,128)S(1)} %advance.1.grid), custom_call_target="tpu_custom_call" | custom-call | tf_op jit(solution)/shard_map/siac_filter/pallas_call | solution.py:370
Async XLA Ops:
  0.6 1.3 %copy-start = (f32[9,64,512]{2,1,0:T(8,128)S(1)}, f32[9,64,512]{2,1,0:T(8,128)}, u32[]{:S(2)}) copy-start(f32[9,64,512]{2,1,0:T(8,128)} %start.1) | copy-start | bytes 3538948
  1.9 1.3 %copy-start.1 = (f32[9,64,512]{2,1,0:T(8,128)S(1)}, f32[9,64,512]{2,1,0:T(8,128)}, u32[]{:S(2)}) copy-start(f32[9,64,512]{2,1,0:T(8,128)} %section.1) | copy-start | bytes 3538948
  3.2 0.9 %copy-start.2 = (f32[64,512]{1,0:T(8,128)S(1)}, f32[64,512]{1,0:T(8,128)}, u32[]{:S(2)}) copy-start(f32[64,512]{1,0:T(8,128)} %vel_x.1) | copy-start | bytes 393220
  4.1 0.9 %copy-start.3 = (f32[64,512]{1,0:T(8,128)S(1)}, f32[64,512]{1,0:T(8,128)}, u32[]{:S(2)}) copy-start(f32[64,512]{1,0:T(8,128)} %vel_y.1) | copy-start | bytes 393220
where the time goes:
time: 22.6 us; the launch traced here: 22.4 us
  Pallas kernels  17.4 us (77%)
  local copies, waits for them, and re-layouts  4.34 us (19%)
  between operations  0.65 us (3%)
    pallas_call x1, Pallas kernels, per_device(): pl.pallas_call(functools.partial(advance_kernel, counts), out_shape=jax.S...  12.9 us
    pallas_call x1, Pallas kernels, per_device(): pl.pallas_call(functools.partial(filter_kernel, table), out_shape=(whole,...  4.46 us
    unnamed x8, local copies, waits for them, and re-layouts  4.34 us

commit v1 on v0

--- a/solution.py
+++ b/solution.py
@@ -191,26 +191,34 @@
             "gy": lax.rem(me_y + (step_y + counts[1]), counts[1]),
         }
 
-    inner = (pl.ds(0, height), pl.ds(0, width))
-    sources = (
-        (section, ext.at[(pl.ds(0, MODES),) + inner]),
-        (start, ext.at[(pl.ds(MODES, MODES),) + inner]),
-        (vel_x, ext.at[(VEL_X,) + inner]),
-        (vel_y, ext.at[(VEL_Y,) + inner]),
-    )
-    loads = [
-        pltpu.make_async_copy(source, target, load_sem.at[index])
-        for index, (source, target) in enumerate(sources)
-    ]
-    for load in loads:
-        load.start()
-
     around = [(i, j) for i in (-1, 0, 1) for j in (-1, 0, 1) if (i, j) != (0, 0)]
     barrier = pltpu.get_barrier_semaphore()
     for i, j in around:
         pl.semaphore_signal(
             barrier, inc=1, device_id=at(i, j), device_id_type=pl.DeviceIdType.MESH
         )
+
+    def load(columns, first_sem):
+        inner = (pl.ds(0, height), columns)
+        sources = (
+            (section.at[:, :, columns], ext.at[(pl.ds(0, MODES),) + inner]),
+            (start.at[:, :, columns], ext.at[(pl.ds(MODES, MODES),) + inner]),
+            (vel_x.at[:, columns], ext.at[(VEL_X,) + inner]),
+            (vel_y.at[:, columns], ext.at[(VEL_Y,) + inner]),
+        )
+        copies = [
+            pltpu.make_async_copy(source, target, load_sem.at[first_sem + index])
+            for index, (source, target) in enumerate(sources)
+        ]
+        for copy in copies:
+            copy.start()
+        return copies
+
+    edge_loads = load(pl.ds(0, LANE), 0) + load(pl.ds(width - LANE, LANE), 4)
+    inner_loads = load(pl.ds(LANE, width - 2 * LANE), 8)
+    for copy in edge_loads:
+        copy.wait()
+    pl.loop(0, tiles - 1)(functools.partial(pack_tile, ext, pack, width))
     pl.semaphore_wait(barrier, len(around))
 
     made = []
@@ -231,30 +239,27 @@
     low, high = pl.ds(0, HALO), pl.ds(height - HALO, HALO)
     north_halo, south_halo = pl.ds(height, HALO), pl.ds(height + SUB - HALO, HALO)
     wide = pl.ds(0, width)
+    whole = pl.ds(0, height)
+    send(pack.at[whole, :], from_west.at[whole, :], at(1, 0))
+    send(pack.at[whole, :], from_east.at[whole, :], at(-1, 0))
+    column_copies = list(made)
+    for rows, halo, step in ((low, north_halo, -1), (high, south_halo, 1)):
+        send(pack.at[rows, :], from_west.at[halo, :], at(1, step))
+        send(pack.at[rows, :], from_east.at[halo, :], at(-1, step))
     for rows, halo, step in ((low, north_halo, -1), (high, south_halo, 1)):
         send(section.at[:, rows, :], ext.at[pl.ds(0, MODES), halo, wide], at(0, step))
         send(start.at[:, rows, :], ext.at[pl.ds(MODES, MODES), halo, wide], at(0, step))
         send(vel_x.at[rows, :], ext.at[VEL_X, halo, wide], at(0, step))
         send(vel_y.at[rows, :], ext.at[VEL_Y, halo, wide], at(0, step))
-    row_copies = list(made)
-
-    for load in loads:
-        load.wait()
-    pl.loop(0, tiles - 1)(functools.partial(pack_tile, ext, pack, width))
-    whole = pl.ds(0, height)
-    send(pack.at[whole, :], from_west.at[whole, :], at(1, 0))
-    send(pack.at[whole, :], from_east.at[whole, :], at(-1, 0))
-    column_copies = made[len(row_copies) :]
-    for rows, halo, step in ((low, north_halo, -1), (high, south_halo, 1)):
-        send(pack.at[rows, :], from_west.at[halo, :], at(1, step))
-        send(pack.at[rows, :], from_east.at[halo, :], at(-1, step))
-    corner_copies = made[len(row_copies) + 2 :]
-
+    row_copies = made[len(column_copies) :]
+
+    for copy in inner_loads:
+        copy.wait()
     for copy in column_copies:
         copy.wait_recv()
     pl.loop(0, tiles - 1)(functools.partial(unpack_tile, ext, from_west, from_east, width))
     pl.loop(1, tiles - 2)(functools.partial(update_tile, ext, out, tiles))
-    for copy in row_copies + corner_copies:
+    for copy in row_copies:
         copy.wait_recv()
     unpack_tile(ext, from_west, from_east, width, tiles - 1)
 
@@ -343,9 +348,13 @@
 def per_device(counts, start_coeffs, section_coeffs, vel_x, vel_y):
     modes, height, width = start_coeffs.shape
     tall, wide = height + SUB, width + LANE
-    anywhere = pl.BlockSpec(memory_space=pl.ANY)
+    anywhere = pl.BlockSpec(memory_space=pltpu.HBM)
     local = pl.BlockSpec(memory_space=pltpu.VMEM)
     messages = 14
+    inputs = [
+        pltpu.with_memory_space_constraint(value, pltpu.HBM)
+        for value in (start_coeffs, section_coeffs, vel_x, vel_y)
+    ]
     grid = pl.pallas_call(
         functools.partial(advance_kernel, counts),
         out_shape=jax.ShapeDtypeStruct((modes, tall, wide), jnp.float32),
@@ -356,7 +365,7 @@
             pltpu.VMEM((height, LANE), jnp.float32),
             pltpu.VMEM((tall, LANE), jnp.float32),
             pltpu.VMEM((tall, LANE), jnp.float32),
-            pltpu.SemaphoreType.DMA((4,)),
+            pltpu.SemaphoreType.DMA((12,)),
             pltpu.SemaphoreType.DMA((messages,)),
             pltpu.SemaphoreType.DMA((messages,)),
         ],
@@ -364,7 +373,7 @@
             collective_id=0, has_side_effects=True, vmem_limit_bytes=VMEM_BYTES
         ),
         name="advance",
-    )(start_coeffs, section_coeffs, vel_x, vel_y)
+    )(*inputs)
     table = [[[float(v) for v in row] for row in part] for part in siac_table().astype(np.float32)]
     whole = jax.ShapeDtypeStruct((modes, height, width), jnp.float32)
     return pl.pallas_call(

time: 22.6 us -> 17.3 us (0.77)
  local copies, waits for them, and re-layouts: 4.34 us -> 0 us
  Pallas kernels: 17.4 us -> 16.5 us
    unnamed x8 -> x0, local copies, waits for them, and re-layouts: 4.34 us -> none
    pallas_call x1, Pallas kernels: 12.9 us -> 12.1 us  [per_device(): pl.pallas_call(functools.partial(advance_kernel, counts), out_shape=jax.S...]
where the time goes in v1:
time: 17.3 us; the launch traced here: 17.2 us
  Pallas kernels  16.5 us (95%)
  between operations  0.64 us (4%)
    pallas_call x1, Pallas kernels, per_device(): pl.pallas_call(functools.partial(advance_kernel, counts), out_shape=jax.S...  12.1 us
    pallas_call x1, Pallas kernels, per_device(): pl.pallas_call(functools.partial(filter_kernel, table), out_shape=(whole,...  4.46 us

profile of v1, /device:TPU:0, one launch (start us, length us, event | category | flops | bytes accessed | tf_op | source)
XLA Modules:
  0.0 17.2 jit_solution(9562467012217085983)
XLA Ops:
  0.6 12.1 %advance.1.grid = f32[9,72,640]{2,1,0:T(8,128)S(1)} custom-call(f32[9,64,512]{2,1,0:T(8,128)} %start.1, f32[9,64,512]{2,1,0:T(8,128)} %section.1, f32[64,512]{1,0:T(8,128)} %vel_x.1, f32[64,512]{1,0:T(8,128)} %vel_y.1), custom_call_target="tpu_custom_call" | custom-call | tf_op jit(solution)/shard_map/advance/pallas_call | solution.py:358
  12.7 4.5 %siac_filter.1 = (f32[9,64,512]{2,1,0:T(8,128)}, f32[9,64,512]{2,1,0:T(8,128)}) custom-call(f32[9,72,640]{2,1,0:T(8,128)S(1)} %advance.1.grid), custom_call_target="tpu_custom_call" | custom-call | tf_op jit(solution)/shard_map/siac_filter/pallas_call | solution.py:379

commit v2 on v1

--- a/solution.py
+++ b/solution.py
@@ -80,6 +80,7 @@
 FIELDS = 2 * MODES + 2
 VEL_X = 2 * MODES
 VEL_Y = 2 * MODES + 1
+UNROLL = 7
 VMEM_BYTES = 40 * 1024 * 1024
 
 
@@ -218,7 +219,7 @@
     inner_loads = load(pl.ds(LANE, width - 2 * LANE), 8)
     for copy in edge_loads:
         copy.wait()
-    pl.loop(0, tiles - 1)(functools.partial(pack_tile, ext, pack, width))
+    pl.loop(0, tiles - 1, unroll=8)(functools.partial(pack_tile, ext, pack, width))
     pl.semaphore_wait(barrier, len(around))
 
     made = []
@@ -257,13 +258,13 @@
         copy.wait()
     for copy in column_copies:
         copy.wait_recv()
-    pl.loop(0, tiles - 1)(functools.partial(unpack_tile, ext, from_west, from_east, width))
-    pl.loop(1, tiles - 2)(functools.partial(update_tile, ext, out, tiles))
+    pl.loop(0, tiles - 1, unroll=8)(functools.partial(unpack_tile, ext, from_west, from_east, width))
+    pl.loop(1, tiles - 2, unroll=6)(functools.partial(update_tile, ext, out, tiles))
     for copy in row_copies:
         copy.wait_recv()
     unpack_tile(ext, from_west, from_east, width, tiles - 1)
 
-    @pl.loop(tiles - 2, tiles + 1)
+    @pl.loop(tiles - 2, tiles + 1, unroll=3)
     def _(tile):
         update_tile(ext, out, tiles, lax.rem(tile, tiles))
 
@@ -302,8 +303,7 @@
     )
     keep.start()
 
-    @pl.loop(0, tiles)
-    def _(tile):
+    def sweep_x(tile):
         rows = rows_of(tile)
         for j in range(3):
             middle = [grid[3 * i + j, rows, :] for i in range(3)]
@@ -312,8 +312,7 @@
             for i in range(3):
                 swept[3 * i + j, rows, :] = sums[i]
 
-    @pl.loop(0, tiles - 1)
-    def _(tile):
+    def sweep_y(tile):
         here = rows_of(tile)
         below = rows_of(lax.rem(tile + (tiles - 1), tiles))
         above = rows_of(tile + 1)
@@ -334,6 +333,16 @@
         pltpu.make_async_copy(
             result.at[:, here, :], filtered.at[:, here, :], out_sem.at[tile]
         ).start()
+
+    sweep_x(tiles - 1)
+    sweep_x(0)
+
+    @pl.loop(0, tiles - 2, unroll=UNROLL)
+    def _(tile):
+        sweep_x(tile + 1)
+        sweep_y(tile)
+
+    sweep_y(tiles - 2)
 
     @pl.loop(0, tiles - 1)
     def _(tile):

time: 17.3 us -> 15.8 us (0.913)
  Pallas kernels: 16.5 us -> 15 us
    pallas_call x1, Pallas kernels: 4.46 us -> 3.24 us  [per_device(): pl.pallas_call(functools.partial(filter_kernel, table), out_shape=(whole,...]
    pallas_call x1, Pallas kernels: 12.1 us -> 11.7 us  [per_device(): pl.pallas_call(functools.partial(advance_kernel, counts), out_shape=jax.S...]
where the time goes in v2:
time: 15.8 us; the launch traced here: 15.6 us
  Pallas kernels  15 us (95%)
  between operations  0.64 us (4%)
    pallas_call x1, Pallas kernels, per_device(): pl.pallas_call(functools.partial(advance_kernel, counts), out_shape=jax.S...  11.7 us
    pallas_call x1, Pallas kernels, per_device(): pl.pallas_call(functools.partial(filter_kernel, table), out_shape=(whole,...  3.24 us

profile of v2, /device:TPU:0, one launch (start us, length us, event | category | flops | bytes accessed | tf_op | source)
XLA Modules:
  0.0 15.6 jit_solution(11848507179881931454)
XLA Ops:
  0.6 11.7 %advance.1.grid = f32[9,72,640]{2,1,0:T(8,128)S(1)} custom-call(f32[9,64,512]{2,1,0:T(8,128)} %start.1, f32[9,64,512]{2,1,0:T(8,128)} %section.1, f32[64,512]{1,0:T(8,128)} %vel_x.1, f32[64,512]{1,0:T(8,128)} %vel_y.1), custom_call_target="tpu_custom_call" | custom-call | tf_op jit(solution)/shard_map/advance/pallas_call | solution.py:367
  12.4 3.2 %siac_filter.1 = (f32[9,64,512]{2,1,0:T(8,128)}, f32[9,64,512]{2,1,0:T(8,128)}) custom-call(f32[9,72,640]{2,1,0:T(8,128)S(1)} %advance.1.grid), custom_call_target="tpu_custom_call" | custom-call | tf_op jit(solution)/shard_map/siac_filter/pallas_call | solution.py:388
